TPU v7x, 128 devices: a whole 4x4x4 slice. The times are simulated.
128 devices in a mesh: dp: 8 (over y, z_hi), ctx: 16 (over x, z_lo, core).
Axes of the slice: x: 4, y: 4, z: 4 (z_hi: 2, z_lo: 2; z = z_hi * 2 + z_lo), core: 2. Of those that a mesh axis runs over, the one named last changes fastest.
Arguments:
- inputs: bfloat16 [8, 2048, 4096], P('dp', 'ctx'), may hold values from -8 to 8
- queries: bfloat16 [8, 2048, 8192], P('dp', 'ctx'), may hold values from -256 to 256
- grad_output: bfloat16 [8, 2048, 8192], P('dp', 'ctx'), may hold values from -6 to 6
- kv_weight: bfloat16 [4096, 1024], P(('dp', 'ctx')), may hold values from -1 to 1
Outputs:
- attn_out: bfloat16 [8, 2048, 8192], P('dp', 'ctx')
- grad_query: bfloat16 [8, 2048, 8192], P('dp', 'ctx')
- grad_inputs: bfloat16 [8, 2048, 4096], P('dp', 'ctx')
- grad_weight: float32 [4096, 1024], P(('dp', 'ctx'))
All inputs are finite; a program needn't handle non-finite values.
Results may differ from a plain program's by a relative error of at most 0.035.
Values may be sent and summed in bfloat16 or wider, within the bound.
A program may use at most 128 MiB of HBM per device.

v0:
```python
import jax
import jax.numpy as jnp
from jax import lax
from jax.sharding import PartitionSpec as P

DH = 128
ROPE_BASE = 500000.0


def shifted(block, axis, distance):
    devices = range(lax.axis_size(axis))
    route = [(i - distance, i) for i in devices if i - distance in devices]
    return lax.ppermute(block, axis, route)


def shifted_2(value, axis, steps):
    count = lax.axis_size(axis)
    pairs = [(source, (source + steps) % count) for source in range(count)]
    return lax.ppermute(value, axis, pairs)


def rope_tables(positions, head_dim):
    half_dim = head_dim // 2
    frequency = ROPE_BASE ** (-2.0 * jnp.arange(half_dim, dtype=jnp.float32) / head_dim)
    angles = positions.astype(jnp.float32)[:, None] * frequency[None, :]
    return (jnp.cos(angles)[:, None, :], jnp.sin(angles)[:, None, :])


def rotary(values, positions):
    half_dim = values.shape[-1] // 2
    cosine, sine_table = rope_tables(positions, values.shape[-1])
    first_half = values[..., :half_dim]
    second = values[..., half_dim:]
    return jnp.concatenate(
        [first_half * cosine - second * sine_table, second * cosine + first_half * sine_table],
        axis=-1,
    )


def rotary_back(gradient, positions):
    half_dim = gradient.shape[-1] // 2
    cosine, sine_table = rope_tables(positions, gradient.shape[-1])
    first_half = gradient[..., :half_dim]
    second = gradient[..., half_dim:]
    return jnp.concatenate(
        [first_half * cosine + second * sine_table, second * cosine - first_half * sine_table],
        axis=-1,
    )


def on_device(inputs, queries, grad_output, kv_weight):
    token_count = inputs.shape[1]
    kv_width = kv_weight.shape[1]
    kv_half = kv_width // 2
    head_dim = DH
    kv_heads = kv_half // head_dim
    q_heads = queries.shape[2] // head_dim
    group_size = q_heads // kv_heads
    row_count = group_size * token_count
    ctx_size = lax.axis_size("ctx")
    ctx_index = lax.axis_index("ctx")
    score_scale = head_dim ** (-0.5)
    tokens = inputs[0]
    weight_all = lax.all_gather(kv_weight, ("dp", "ctx"), axis=0, tiled=True)
    projected = jnp.dot(tokens, weight_all, preferred_element_type=jnp.float32)
    positions = ctx_index * token_count + jnp.arange(token_count, dtype=jnp.int32)
    key_rows = rotary(
        projected[:, :kv_half].reshape(token_count, kv_heads, head_dim), positions
    ).astype(jnp.bfloat16)
    value_rows = projected[:, kv_half:].astype(jnp.bfloat16)
    own_block = jnp.concatenate([key_rows.reshape(token_count, kv_half), value_rows], axis=1)

    def head_rows(matrix):
        return (
            matrix.reshape(token_count, kv_heads, group_size, head_dim)
            .transpose(1, 2, 0, 3)
            .reshape(kv_heads, row_count, head_dim)
        )

    def token_rows(rows_by_head):
        return (
            rows_by_head.reshape(kv_heads, group_size, token_count, head_dim)
            .transpose(2, 0, 1, 3)
            .reshape(token_count, q_heads * head_dim)
        )

    query_rows = head_rows(queries[0])
    grad_rows = head_rows(grad_output[0])
    query_pos = jnp.arange(row_count, dtype=jnp.int32) % token_count
    key_pos = jnp.arange(token_count, dtype=jnp.int32)

    def split_block(kv_block):
        key_part = kv_block[:, :kv_half].reshape(token_count, kv_heads, head_dim)
        value_part = kv_block[:, kv_half:].reshape(token_count, kv_heads, head_dim)
        return (key_part, value_part)

    def block_scores(key_part, block_id):
        scores = (
            jnp.einsum("hrd,khd->hrk", query_rows, key_part, preferred_element_type=jnp.float32)
            * score_scale
        )
        allowed = (block_id < ctx_index) | (query_pos[:, None] >= key_pos[None, :])
        return (scores, allowed)

    def forward_update(state_now, kv_block, block_id):
        row_top, row_total, row_accum = state_now
        key_part, value_part = split_block(kv_block)
        scores, allowed = block_scores(key_part, block_id)
        scores = jnp.where(allowed[None], scores, -jnp.inf)
        new_top = jnp.maximum(row_top, jnp.max(scores, axis=-1, keepdims=True))
        weights = jnp.exp(scores - new_top)
        factor = jnp.exp(row_top - new_top)
        row_total = row_total * factor + jnp.sum(weights, axis=-1, keepdims=True)
        row_accum = row_accum * factor + jnp.einsum(
            "hrk,khd->hrd",
            weights.astype(jnp.bfloat16),
            value_part,
            preferred_element_type=jnp.float32,
        )
        return (new_top, row_total, row_accum)

    start_state = (
        jnp.full((kv_heads, row_count, 1), -jnp.inf, jnp.float32),
        jnp.zeros((kv_heads, row_count, 1), jnp.float32),
        jnp.zeros((kv_heads, row_count, head_dim), jnp.float32),
    )
    state_now = forward_update(start_state, own_block, ctx_index)
    kv_store = jnp.zeros((ctx_size, token_count, kv_width), jnp.bfloat16)
    kv_store = lax.dynamic_update_slice_in_dim(kv_store, own_block[None], ctx_index, 0)

    def forward_step(offset, loop_state):
        kv_block, stored_now, state_here = loop_state
        kv_block = shifted(kv_block, "ctx", 1)
        source = ctx_index - offset

        def take_block(operands):
            stored, current = operands
            stored = lax.dynamic_update_slice_in_dim(stored, kv_block[None], source, 0)
            return (stored, forward_update(current, kv_block, source))

        def keep_state(operands):
            return operands

        stored_now, state_here = lax.cond(
            offset <= ctx_index, take_block, keep_state, (stored_now, state_here)
        )
        return (kv_block, stored_now, state_here)

    last_block, kv_store, state_now = lax.fori_loop(
        1, ctx_size, forward_step, (own_block, kv_store, state_now)
    )
    row_top, row_total, row_accum = state_now
    attn_rows = (row_accum / row_total).astype(jnp.bfloat16)
    log_total = row_top + jnp.log(row_total)
    row_delta = jnp.sum(
        grad_rows.astype(jnp.float32) * attn_rows.astype(jnp.float32), axis=-1, keepdims=True
    )
    attn_out = token_rows(attn_rows)[None]

    def backward_terms(kv_block, block_id):
        key_part, value_part = split_block(kv_block)
        scores, allowed = block_scores(key_part, block_id)
        probs_now = jnp.where(allowed[None], jnp.exp(scores - log_total), 0.0)
        dprobs = jnp.einsum(
            "hrd,khd->hrk", grad_rows, value_part, preferred_element_type=jnp.float32
        )
        dscores = (probs_now * (dprobs - row_delta)).astype(jnp.bfloat16)
        grad_keys = (
            jnp.einsum("hrk,hrd->khd", dscores, query_rows, preferred_element_type=jnp.float32)
            * score_scale
        )
        grad_values = jnp.einsum(
            "hrk,hrd->khd",
            probs_now.astype(jnp.bfloat16),
            grad_rows,
            preferred_element_type=jnp.float32,
        )
        query_part = jnp.einsum(
            "hrk,khd->hrd", dscores, key_part, preferred_element_type=jnp.float32
        )
        block_grads = jnp.concatenate(
            [grad_keys.reshape(token_count, kv_half), grad_values.reshape(token_count, kv_half)],
            axis=1,
        )
        return (block_grads, query_part)

    def add_block(operands, block_id):
        grad_block, grad_query_sum = operands
        kv_block = lax.dynamic_slice_in_dim(kv_store, block_id, 1, 0)[0]
        block_grads, query_part = backward_terms(kv_block, block_id)
        return (grad_block + block_grads, grad_query_sum + query_part)

    def skip_block(operand_pair):
        return operand_pair

    zero_grads = jnp.zeros((token_count, kv_width), jnp.float32)
    zero_query = jnp.zeros((kv_heads, row_count, head_dim), jnp.float32)

    def backward_step(offset, operands):
        source = ctx_index - offset

        def include(operand_pair):
            return add_block(operand_pair, source)

        grad_block, grad_query_sum = lax.cond(offset <= ctx_index, include, skip_block, operands)
        grad_block = shifted_2(grad_block.astype(jnp.bfloat16), "ctx", 1).astype(grad_block.dtype)
        return (grad_block, grad_query_sum)

    grad_block, grad_query_sum = lax.fori_loop(0, ctx_size, backward_step, (zero_grads, zero_query))
    grad_query = token_rows(grad_query_sum * score_scale).astype(jnp.bfloat16)[None]
    grad_key_rows = rotary_back(
        grad_block[:, :kv_half].reshape(token_count, kv_heads, head_dim), positions
    ).reshape(token_count, kv_half)
    grad_projected = jnp.concatenate([grad_key_rows, grad_block[:, kv_half:]], axis=1).astype(
        jnp.bfloat16
    )
    grad_inputs = lax.dot_general(
        grad_projected, weight_all, (((1,), (1,)), ((), ())), preferred_element_type=jnp.float32
    ).astype(jnp.bfloat16)[None]
    grad_weight = lax.psum_scatter(
        lax.dot_general(
            tokens, grad_projected, (((0,), (0,)), ((), ())), preferred_element_type=jnp.float32
        ),
        ("dp", "ctx"),
        scatter_dimension=0,
        tiled=True,
    )
    return (attn_out, grad_query, grad_inputs, grad_weight)


def solution(mesh):
    in_specs = (
        P("dp", "ctx", None),
        P("dp", "ctx", None),
        P("dp", "ctx", None),
        P(("dp", "ctx"), None),
    )
    out_specs = (
        P("dp", "ctx", None),
        P("dp", "ctx", None),
        P("dp", "ctx", None),
        P(("dp", "ctx"), None),
    )
    return jax.shard_map(
        on_device, mesh=mesh, in_specs=in_specs, out_specs=out_specs, check_vma=False
    )
```

profile of v0, /device:TPU:0, one launch (start us, length us, event | category | flops | bytes accessed | tf_op | source)
XLA Modules:
  0.0 1567.8 jit_solution(14216864717612839760)
XLA Ops:
  10.2 3.8 copy.71
  22.9 5.1 copy.79
  28.0 4.2 reshape.237
  33.4 182.2 %all-gather.2.cloned.1.call-done = bf16[4096,1024]{1,0:T(8,128)(2,1)} async-done(((bf16[32,1024]{1,0:T(8,128)(2,1)}), bf16[4096,1024]{1,0:T(8,128)(2,1)}) %all-gather.2.cloned.1.call-update) | async-done | bytes 8388624 | tf_op jit(solution)/shard_map/all_gather | solution.py:64
  215.6 4.6 fusion.28
  237.7 180.0 %while.38 = (s32[]{:T(128)}, bf16[128,1024]{0,1:T(8,128)(2,1)}, bf16[16,128,1024]{1,2,0:T(8,128)(2,1)}, f32[4,2048,1]{1,0,2:T(4,128)S(1)}, f32[4,2048,1]{1,0,2:T...) while((s32[]{:T(128)}, bf16[128,1024]{0,1:T(8,128)(2,1)}, ...), condition=%wide.region_7.8_spmd.clone, body=%wide.region_2.7_spmd.clone.sunk | while | flops 551063552 | bytes 61154760 | solution.py:149
  241.1 15.3 collective-permute-start
  258.4 6.5 collective-permute-start
  267.0 16.2 %collective-permute-start = (bf16[128,1024]{0,1:T(8,128)(2,1)}, bf16[128,1024]{0,1:T(8,128)(2,1)S(1)}, u32[]{:S(2)}, u32[]{:S(2)}) collective-permute-start(bf16[128,1024]{0,1:T(8,128)(2,1)} %get-tuple-element.838), channel_id=1, source_target_pairs={{0,1},{1,2},{2,3},{3,4},{4,5},{5,6},{6,7},{7,8},{8,9},{9,10},{10,1... | collective-permute-start | bytes 786440 | tf_op jit(solution)/shard_map/while/body/eval_jaxpr/ppermute | solution.py:13
  285.3 6.5 collective-permute-start
  293.9 12.5 collective-permute-start
  308.4 7.5 collective-permute-start
  318.0 17.1 %collective-permute-start = (bf16[128,1024]{0,1:T(8,128)(2,1)}, bf16[128,1024]{0,1:T(8,128)(2,1)S(1)}, u32[]{:S(2)}, u32[]{:S(2)}) collective-permute-start(bf16[128,1024]{0,1:T(8,128)(2,1)} %get-tuple-element.838), channel_id=1, source_target_pairs={{0,1},{1,2},{2,3},{3,4},{4,5},{5,6},{6,7},{7,8},{8,9},{9,10},{10,1... | collective-permute-start | bytes 786440 | tf_op jit(solution)/shard_map/while/body/eval_jaxpr/ppermute | solution.py:13
  337.1 7.4 collective-permute-start
  346.6 7.4 collective-permute-start
  356.1 7.4 collective-permute-start
  365.6 13.7 collective-permute-start
  381.3 7.4 collective-permute-start
  390.8 15.3 collective-permute-start
  408.2 7.4 collective-permute-start
  417.7 5.4 copy.77
  423.1 5.0 multiply_reduce_fusion
  430.3 439.3 %while.39 = (s32[]{:T(128)}, f32[128,1024]{0,1:T(8,128)}, f32[4,2048,128]{2,1,0:T(8,128)}, s32[]{:T(128)}, bf16[16,128,1024]{1,2,0:T(8,128)(2,1)}, /*index=5*/bf...) while((s32[]{:T(128)}, f32[128,1024]{0,1:T(8,128)}, ...), condition=%wide.region_12.13_spmd.clone, body=%wide.region_9.12_spmd.clone.sunk | while | flops 1351823360 | bytes 85468640 | solution.py:209
  431.1 11.4 conditional.7
  443.6 15.2 collective-permute-start.1
  458.9 85.0 %collective-permute-done.1 = bf16[128,1024]{0,1:T(8,128)(2,1)} collective-permute-done((bf16[128,1024]{0,1:T(8,128)(2,1)S(1)}, bf16[128,1024]{0,1:T(8,128)(2,1)}, u32[]{:S(2)}, u32[]{:S(2)}) %collective-permute-start.1) | collective-permute-done | bytes 262176 | tf_op jit(solution)/shard_map/while/body/eval_jaxpr/ppermute | solution.py:19
  548.7 14.7 collective-permute-done.1
  568.3 14.7 collective-permute-done.1
  587.9 14.7 collective-permute-done.1
  607.5 16.2 %collective-permute-done.1 = bf16[128,1024]{0,1:T(8,128)(2,1)} collective-permute-done((bf16[128,1024]{0,1:T(8,128)(2,1)S(1)}, bf16[128,1024]{0,1:T(8,128)(2,1)}, u32[]{:S(2)}, u32[]{:S(2)}) %collective-permute-start.1) | collective-permute-done | bytes 262176 | tf_op jit(solution)/shard_map/while/body/eval_jaxpr/ppermute | solution.py:19
  628.6 17.3 %collective-permute-done.1 = bf16[128,1024]{0,1:T(8,128)(2,1)} collective-permute-done((bf16[128,1024]{0,1:T(8,128)(2,1)S(1)}, bf16[128,1024]{0,1:T(8,128)(2,1)}, u32[]{:S(2)}, u32[]{:S(2)}) %collective-permute-start.1) | collective-permute-done | bytes 262176 | tf_op jit(solution)/shard_map/while/body/eval_jaxpr/ppermute | solution.py:19
  650.8 17.3 %collective-permute-done.1 = bf16[128,1024]{0,1:T(8,128)(2,1)} collective-permute-done((bf16[128,1024]{0,1:T(8,128)(2,1)S(1)}, bf16[128,1024]{0,1:T(8,128)(2,1)}, u32[]{:S(2)}, u32[]{:S(2)}) %collective-permute-start.1) | collective-permute-done | bytes 262176 | tf_op jit(solution)/shard_map/while/body/eval_jaxpr/ppermute | solution.py:19
  673.0 17.3 %collective-permute-done.1 = bf16[128,1024]{0,1:T(8,128)(2,1)} collective-permute-done((bf16[128,1024]{0,1:T(8,128)(2,1)S(1)}, bf16[128,1024]{0,1:T(8,128)(2,1)}, u32[]{:S(2)}, u32[]{:S(2)}) %collective-permute-start.1) | collective-permute-done | bytes 262176 | tf_op jit(solution)/shard_map/while/body/eval_jaxpr/ppermute | solution.py:19
  695.2 17.3 %collective-permute-done.1 = bf16[128,1024]{0,1:T(8,128)(2,1)} collective-permute-done((bf16[128,1024]{0,1:T(8,128)(2,1)S(1)}, bf16[128,1024]{0,1:T(8,128)(2,1)}, u32[]{:S(2)}, u32[]{:S(2)}) %collective-permute-start.1) | collective-permute-done | bytes 262176 | tf_op jit(solution)/shard_map/while/body/eval_jaxpr/ppermute | solution.py:19
  717.4 17.3 %collective-permute-done.1 = bf16[128,1024]{0,1:T(8,128)(2,1)} collective-permute-done((bf16[128,1024]{0,1:T(8,128)(2,1)S(1)}, bf16[128,1024]{0,1:T(8,128)(2,1)}, u32[]{:S(2)}, u32[]{:S(2)}) %collective-permute-start.1) | collective-permute-done | bytes 262176 | tf_op jit(solution)/shard_map/while/body/eval_jaxpr/ppermute | solution.py:19
  739.6 17.3 %collective-permute-done.1 = bf16[128,1024]{0,1:T(8,128)(2,1)} collective-permute-done((bf16[128,1024]{0,1:T(8,128)(2,1)S(1)}, bf16[128,1024]{0,1:T(8,128)(2,1)}, u32[]{:S(2)}, u32[]{:S(2)}) %collective-permute-start.1) | collective-permute-done | bytes 262176 | tf_op jit(solution)/shard_map/while/body/eval_jaxpr/ppermute | solution.py:19
  761.7 17.3 %collective-permute-done.1 = bf16[128,1024]{0,1:T(8,128)(2,1)} collective-permute-done((bf16[128,1024]{0,1:T(8,128)(2,1)S(1)}, bf16[128,1024]{0,1:T(8,128)(2,1)}, u32[]{:S(2)}, u32[]{:S(2)}) %collective-permute-start.1) | collective-permute-done | bytes 262176 | tf_op jit(solution)/shard_map/while/body/eval_jaxpr/ppermute | solution.py:19
  783.9 17.3 %collective-permute-done.1 = bf16[128,1024]{0,1:T(8,128)(2,1)} collective-permute-done((bf16[128,1024]{0,1:T(8,128)(2,1)S(1)}, bf16[128,1024]{0,1:T(8,128)(2,1)}, u32[]{:S(2)}, u32[]{:S(2)}) %collective-permute-start.1) | collective-permute-done | bytes 262176 | tf_op jit(solution)/shard_map/while/body/eval_jaxpr/ppermute | solution.py:19
  806.1 17.3 %collective-permute-done.1 = bf16[128,1024]{0,1:T(8,128)(2,1)} collective-permute-done((bf16[128,1024]{0,1:T(8,128)(2,1)S(1)}, bf16[128,1024]{0,1:T(8,128)(2,1)}, u32[]{:S(2)}, u32[]{:S(2)}) %collective-permute-start.1) | collective-permute-done | bytes 262176 | tf_op jit(solution)/shard_map/while/body/eval_jaxpr/ppermute | solution.py:19
  828.3 17.3 %collective-permute-done.1 = bf16[128,1024]{0,1:T(8,128)(2,1)} collective-permute-done((bf16[128,1024]{0,1:T(8,128)(2,1)S(1)}, bf16[128,1024]{0,1:T(8,128)(2,1)}, u32[]{:S(2)}, u32[]{:S(2)}) %collective-permute-start.1) | collective-permute-done | bytes 262176 | tf_op jit(solution)/shard_map/while/body/eval_jaxpr/ppermute | solution.py:19
  850.5 17.3 %collective-permute-done.1 = bf16[128,1024]{0,1:T(8,128)(2,1)} collective-permute-done((bf16[128,1024]{0,1:T(8,128)(2,1)S(1)}, bf16[128,1024]{0,1:T(8,128)(2,1)}, u32[]{:S(2)}, u32[]{:S(2)}) %collective-permute-start.1) | collective-permute-done | bytes 262176 | tf_op jit(solution)/shard_map/while/body/eval_jaxpr/ppermute | solution.py:19
  873.1 8.1 convolution_bitcast_fusion
  881.2 17.4 %copy.98 = f32[4096,1024]{1,0:T(8,128)} copy(f32[4096,1024]{0,1:T(8,128)} %convolution_bitcast_fusion) | data formatting | bytes 33554432
  900.8 3.8 copy.78
  904.6 4.2 broadcast_in_dim_reshape.3
  914.1 4.2 convert_element_type.98
  918.2 7.2 fusion.22
  925.5 635.5 %reduce-scatter.4.cloned.1.call-done = f32[32,1024]{1,0:T(8,128)} async-done(((f32[4096,1024]{1,0:T(8,128)}), f32[32,1024]{1,0:T(8,128)}) %reduce-scatter.4.cloned.1.call-update) | async-done | bytes 131088
  (290 shorter events, 163.3 us)
Async XLA Ops:
  7.2 208.4 %copy-start = (bf16[1,128,4096]{2,1,0:T(8,128)(2,1)S(1)}, bf16[1,128,4096]{2,1,0:T(8,128)(2,1)}, u32[]{:S(2)}) copy-start(bf16[1,128,4096]{2,1,0:T(8,128)(2,1)} %param.12) | copy-start | bytes 3145732
  7.2 208.4 %all-gather.2.cloned.1.call-start = ((), (), s32[]{:S(2)}) async-start(), calls=%async_computation.1 | async-start | bytes 8454144 | tf_op jit(solution)/shard_map/all_gather | solution.py:64
  7.9 1553.0 %reduce-scatter.4.cloned.1.call-start = ((), (), s32[]{:S(2)}) async-start(), calls=%async_computation.2 | async-start | bytes 16908288
  32.5 190.6 %copy-start.10 = (f32[128,64]{1,0:T(8,128)}, f32[128,64]{1,0:T(8,128)S(1)}, u32[]{:S(2)}) copy-start(f32[128,64]{1,0:T(8,128)S(1)} %get-tuple-element.695) | copy-start | bytes 98308
  32.5 190.5 %copy-start.11 = (f32[128,64]{1,0:T(8,128)}, f32[128,64]{1,0:T(8,128)S(1)}, u32[]{:S(2)}) copy-start(f32[128,64]{1,0:T(8,128)S(1)} %get-tuple-element.696) | copy-start | bytes 98308
  220.2 0.8 copy-start.7
  228.6 2.9 copy-start.8
  234.7 0.9 copy-start.9
  235.7 2.0 copy-start.6
  237.7 2.7 collective-permute-start
  241.1 16.7 %collective-permute-start = (bf16[128,1024]{0,1:T(8,128)(2,1)}, bf16[128,1024]{0,1:T(8,128)(2,1)S(1)}, u32[]{:S(2)}, u32[]{:S(2)}) collective-permute-start(bf16[128,1024]{0,1:T(8,128)(2,1)} %get-tuple-element.838), channel_id=1, source_target_pairs={{0,1},{1,2},{2,3},{3,4},{4,5},{5,6},{6,7},{7,8},{8,9},{9,10},{10,1... | collective-permute-start | bytes 786440 | tf_op jit(solution)/shard_map/while/body/eval_jaxpr/ppermute | solution.py:13
  258.4 7.9 collective-permute-start
  267.0 17.5 %collective-permute-start = (bf16[128,1024]{0,1:T(8,128)(2,1)}, bf16[128,1024]{0,1:T(8,128)(2,1)S(1)}, u32[]{:S(2)}, u32[]{:S(2)}) collective-permute-start(bf16[128,1024]{0,1:T(8,128)(2,1)} %get-tuple-element.838), channel_id=1, source_target_pairs={{0,1},{1,2},{2,3},{3,4},{4,5},{5,6},{6,7},{7,8},{8,9},{9,10},{10,1... | collective-permute-start | bytes 786440 | tf_op jit(solution)/shard_map/while/body/eval_jaxpr/ppermute | solution.py:13
  285.3 7.9 collective-permute-start
  293.9 13.9 collective-permute-start
  308.4 8.8 collective-permute-start
  318.0 18.4 %collective-permute-start = (bf16[128,1024]{0,1:T(8,128)(2,1)}, bf16[128,1024]{0,1:T(8,128)(2,1)S(1)}, u32[]{:S(2)}, u32[]{:S(2)}) collective-permute-start(bf16[128,1024]{0,1:T(8,128)(2,1)} %get-tuple-element.838), channel_id=1, source_target_pairs={{0,1},{1,2},{2,3},{3,4},{4,5},{5,6},{6,7},{7,8},{8,9},{9,10},{10,1... | collective-permute-start | bytes 786440 | tf_op jit(solution)/shard_map/while/body/eval_jaxpr/ppermute | solution.py:13
  337.1 8.8 collective-permute-start
  346.6 8.8 collective-permute-start
  356.1 8.8 collective-permute-start
  365.6 15.0 collective-permute-start
  381.3 8.8 collective-permute-start
  390.8 16.7 %collective-permute-start = (bf16[128,1024]{0,1:T(8,128)(2,1)}, bf16[128,1024]{0,1:T(8,128)(2,1)S(1)}, u32[]{:S(2)}, u32[]{:S(2)}) collective-permute-start(bf16[128,1024]{0,1:T(8,128)(2,1)} %get-tuple-element.838), channel_id=1, source_target_pairs={{0,1},{1,2},{2,3},{3,4},{4,5},{5,6},{6,7},{7,8},{8,9},{9,10},{10,1... | collective-permute-start | bytes 786440 | tf_op jit(solution)/shard_map/while/body/eval_jaxpr/ppermute | solution.py:13
  408.2 8.8 collective-permute-start
  431.1 2.8 copy-start.1
  435.4 3.0 copy-start.4
  440.6 1.9 copy-start.5
  443.6 100.2 %collective-permute-start.1 = (bf16[128,1024]{0,1:T(8,128)(2,1)S(1)}, bf16[128,1024]{0,1:T(8,128)(2,1)}, u32[]{:S(2)}, u32[]{:S(2)}) collective-permute-start(bf16[128,1024]{0,1:T(8,128)(2,1)S(1)} %convert_element_type.130), channel_id=1, source_target_pairs={{0,1},{1,2},{2,3},{3,4},{4,5},{5,6},{6,7},{7,8},{8,9},{9,10},{10,1... | collective-permute-start | bytes 786440 | tf_op jit(solution)/shard_map/while/body/eval_jaxpr/ppermute | solution.py:19
  548.6 14.8 collective-permute-start.1
  568.2 14.8 collective-permute-start.1
  587.8 14.8 collective-permute-start.1
  607.4 16.3 %collective-permute-start.1 = (bf16[128,1024]{0,1:T(8,128)(2,1)S(1)}, bf16[128,1024]{0,1:T(8,128)(2,1)}, u32[]{:S(2)}, u32[]{:S(2)}) collective-permute-start(bf16[128,1024]{0,1:T(8,128)(2,1)S(1)} %convert_element_type.130), channel_id=1, source_target_pairs={{0,1},{1,2},{2,3},{3,4},{4,5},{5,6},{6,7},{7,8},{8,9},{9,10},{10,1... | collective-permute-start | bytes 786440 | tf_op jit(solution)/shard_map/while/body/eval_jaxpr/ppermute | solution.py:19
  628.5 17.4 %collective-permute-start.1 = (bf16[128,1024]{0,1:T(8,128)(2,1)S(1)}, bf16[128,1024]{0,1:T(8,128)(2,1)}, u32[]{:S(2)}, u32[]{:S(2)}) collective-permute-start(bf16[128,1024]{0,1:T(8,128)(2,1)S(1)} %convert_element_type.130), channel_id=1, source_target_pairs={{0,1},{1,2},{2,3},{3,4},{4,5},{5,6},{6,7},{7,8},{8,9},{9,10},{10,1... | collective-permute-start | bytes 786440 | tf_op jit(solution)/shard_map/while/body/eval_jaxpr/ppermute | solution.py:19
  650.7 17.4 %collective-permute-start.1 = (bf16[128,1024]{0,1:T(8,128)(2,1)S(1)}, bf16[128,1024]{0,1:T(8,128)(2,1)}, u32[]{:S(2)}, u32[]{:S(2)}) collective-permute-start(bf16[128,1024]{0,1:T(8,128)(2,1)S(1)} %convert_element_type.130), channel_id=1, source_target_pairs={{0,1},{1,2},{2,3},{3,4},{4,5},{5,6},{6,7},{7,8},{8,9},{9,10},{10,1... | collective-permute-start | bytes 786440 | tf_op jit(solution)/shard_map/while/body/eval_jaxpr/ppermute | solution.py:19
  672.9 17.4 %collective-permute-start.1 = (bf16[128,1024]{0,1:T(8,128)(2,1)S(1)}, bf16[128,1024]{0,1:T(8,128)(2,1)}, u32[]{:S(2)}, u32[]{:S(2)}) collective-permute-start(bf16[128,1024]{0,1:T(8,128)(2,1)S(1)} %convert_element_type.130), channel_id=1, source_target_pairs={{0,1},{1,2},{2,3},{3,4},{4,5},{5,6},{6,7},{7,8},{8,9},{9,10},{10,1... | collective-permute-start | bytes 786440 | tf_op jit(solution)/shard_map/while/body/eval_jaxpr/ppermute | solution.py:19
  695.1 17.4 %collective-permute-start.1 = (bf16[128,1024]{0,1:T(8,128)(2,1)S(1)}, bf16[128,1024]{0,1:T(8,128)(2,1)}, u32[]{:S(2)}, u32[]{:S(2)}) collective-permute-start(bf16[128,1024]{0,1:T(8,128)(2,1)S(1)} %convert_element_type.130), channel_id=1, source_target_pairs={{0,1},{1,2},{2,3},{3,4},{4,5},{5,6},{6,7},{7,8},{8,9},{9,10},{10,1... | collective-permute-start | bytes 786440 | tf_op jit(solution)/shard_map/while/body/eval_jaxpr/ppermute | solution.py:19
  717.3 17.4 %collective-permute-start.1 = (bf16[128,1024]{0,1:T(8,128)(2,1)S(1)}, bf16[128,1024]{0,1:T(8,128)(2,1)}, u32[]{:S(2)}, u32[]{:S(2)}) collective-permute-start(bf16[128,1024]{0,1:T(8,128)(2,1)S(1)} %convert_element_type.130), channel_id=1, source_target_pairs={{0,1},{1,2},{2,3},{3,4},{4,5},{5,6},{6,7},{7,8},{8,9},{9,10},{10,1... | collective-permute-start | bytes 786440 | tf_op jit(solution)/shard_map/while/body/eval_jaxpr/ppermute | solution.py:19
  739.5 17.4 %collective-permute-start.1 = (bf16[128,1024]{0,1:T(8,128)(2,1)S(1)}, bf16[128,1024]{0,1:T(8,128)(2,1)}, u32[]{:S(2)}, u32[]{:S(2)}) collective-permute-start(bf16[128,1024]{0,1:T(8,128)(2,1)S(1)} %convert_element_type.130), channel_id=1, source_target_pairs={{0,1},{1,2},{2,3},{3,4},{4,5},{5,6},{6,7},{7,8},{8,9},{9,10},{10,1... | collective-permute-start | bytes 786440 | tf_op jit(solution)/shard_map/while/body/eval_jaxpr/ppermute | solution.py:19
  761.7 17.4 %collective-permute-start.1 = (bf16[128,1024]{0,1:T(8,128)(2,1)S(1)}, bf16[128,1024]{0,1:T(8,128)(2,1)}, u32[]{:S(2)}, u32[]{:S(2)}) collective-permute-start(bf16[128,1024]{0,1:T(8,128)(2,1)S(1)} %convert_element_type.130), channel_id=1, source_target_pairs={{0,1},{1,2},{2,3},{3,4},{4,5},{5,6},{6,7},{7,8},{8,9},{9,10},{10,1... | collective-permute-start | bytes 786440 | tf_op jit(solution)/shard_map/while/body/eval_jaxpr/ppermute | solution.py:19
  783.9 17.4 %collective-permute-start.1 = (bf16[128,1024]{0,1:T(8,128)(2,1)S(1)}, bf16[128,1024]{0,1:T(8,128)(2,1)}, u32[]{:S(2)}, u32[]{:S(2)}) collective-permute-start(bf16[128,1024]{0,1:T(8,128)(2,1)S(1)} %convert_element_type.130), channel_id=1, source_target_pairs={{0,1},{1,2},{2,3},{3,4},{4,5},{5,6},{6,7},{7,8},{8,9},{9,10},{10,1... | collective-permute-start | bytes 786440 | tf_op jit(solution)/shard_map/while/body/eval_jaxpr/ppermute | solution.py:19
  806.0 17.4 %collective-permute-start.1 = (bf16[128,1024]{0,1:T(8,128)(2,1)S(1)}, bf16[128,1024]{0,1:T(8,128)(2,1)}, u32[]{:S(2)}, u32[]{:S(2)}) collective-permute-start(bf16[128,1024]{0,1:T(8,128)(2,1)S(1)} %convert_element_type.130), channel_id=1, source_target_pairs={{0,1},{1,2},{2,3},{3,4},{4,5},{5,6},{6,7},{7,8},{8,9},{9,10},{10,1... | collective-permute-start | bytes 786440 | tf_op jit(solution)/shard_map/while/body/eval_jaxpr/ppermute | solution.py:19
  828.2 17.4 %collective-permute-start.1 = (bf16[128,1024]{0,1:T(8,128)(2,1)S(1)}, bf16[128,1024]{0,1:T(8,128)(2,1)}, u32[]{:S(2)}, u32[]{:S(2)}) collective-permute-start(bf16[128,1024]{0,1:T(8,128)(2,1)S(1)} %convert_element_type.130), channel_id=1, source_target_pairs={{0,1},{1,2},{2,3},{3,4},{4,5},{5,6},{6,7},{7,8},{8,9},{9,10},{10,1... | collective-permute-start | bytes 786440 | tf_op jit(solution)/shard_map/while/body/eval_jaxpr/ppermute | solution.py:19
  850.4 17.4 %collective-permute-start.1 = (bf16[128,1024]{0,1:T(8,128)(2,1)S(1)}, bf16[128,1024]{0,1:T(8,128)(2,1)}, u32[]{:S(2)}, u32[]{:S(2)}) collective-permute-start(bf16[128,1024]{0,1:T(8,128)(2,1)S(1)} %convert_element_type.130), channel_id=1, source_target_pairs={{0,1},{1,2},{2,3},{3,4},{4,5},{5,6},{6,7},{7,8},{8,9},{9,10},{10,1... | collective-permute-start | bytes 786440 | tf_op jit(solution)/shard_map/while/body/eval_jaxpr/ppermute | solution.py:19
Sparse Core Ops, SparseCore 0:
  9.7 205.8 all-gather.1
  898.7 662.1 reduce-scatter.3
where the time goes:
time: 1570 us
  waiting for transfers between devices  1170 us (75%)
  starting transfers between devices  166 us (11%)
  local copies, waits for them, and re-layouts  91.6 us (6%)
  other arithmetic  90.5 us (6%)
  matrix products  31.1 us (2%)
    unnamed x3, waiting for transfers between devices  636 us
    ppermute x16, waiting for transfers between devices, shifted_2(): return lax.ppermute(value, axis, pairs)  336 us
    all_gather x1, waiting for transfers between devices, on_device(): weight_all = lax.all_gather(kv_weight, ('dp', 'ctx'), axis=0, tiled=True)  182 us
    ppermute x15, starting transfers between devices, shifted(): return lax.ppermute(block, axis, route)  149 us
    unnamed x22, local copies, waits for them, and re-layouts  32.2 us
  transfers between devices with their start and end apart: 33, of which 33 were waited for; matrix products, arithmetic and copies ran while one was open for 3% of the time, Pallas kernels for 0%

commit v1 on v0

--- a/solution.py
+++ b/solution.py
@@ -61,7 +61,10 @@
     ctx_index = lax.axis_index("ctx")
     score_scale = head_dim ** (-0.5)
     tokens = inputs[0]
-    weight_all = lax.all_gather(kv_weight, ("dp", "ctx"), axis=0, tiled=True)
+    weight_all = jnp.concatenate(
+        lax.all_to_all(jnp.stack([kv_weight] * lax.axis_size(("dp", "ctx"))), ("dp", "ctx"), 0, 0),
+        axis=0,
+    )
     projected = jnp.dot(tokens, weight_all, preferred_element_type=jnp.float32)
     positions = ctx_index * token_count + jnp.arange(token_count, dtype=jnp.int32)
     key_rows = rotary(

time: 1570 us -> 1490 us (0.949)
  waiting for transfers between devices: 1170 us -> 1060 us
  starting transfers between devices: 166 us -> 188 us
    all_gather x1 -> x0, waiting for transfers between devices: 182 us -> none  [on_device(): weight_all = lax.all_gather(kv_weight, ('dp', 'ctx'), axis=0, tiled=True)]
    all_to_all x0 -> x1, waiting for transfers between devices: none -> 75.7 us  [on_device(): lax.all_to_all(jnp.stack([kv_weight] * lax.axis_size(('dp', 'ctx'))), ('d...]
    unnamed x3 -> x2, waiting for transfers between devices: 636 us -> 635 us
  transfers between devices with their start and end apart: 33 -> 33, of which waited for: 33 -> 33; matrix products, arithmetic and copies ran while one was open for 3% -> 4% of each run, Pallas kernels for 0% -> 0%
where the time goes in v1:
time: 1490 us; the launch traced here: 1480 us
  waiting for transfers between devices  1060 us (71%)
  starting transfers between devices  188 us (13%)
  local copies, waits for them, and re-layouts  96.8 us (6%)
  other arithmetic  90.4 us (6%)
  matrix products  31.2 us (2%)
    unnamed x2, waiting for transfers between devices  635 us
    ppermute x16, waiting for transfers between devices, shifted_2(): return lax.ppermute(value, axis, pairs)  333 us
    ppermute x15, starting transfers between devices, shifted(): return lax.ppermute(block, axis, route)  160 us
    all_to_all x1, waiting for transfers between devices, on_device(): lax.all_to_all(jnp.stack([kv_weight] * lax.axis_size(('dp', 'ctx'))), ('d...  75.7 us
    unnamed x22, local copies, waits for them, and re-layouts  32.1 us
  transfers between devices with their start and end apart: 33, of which 33 were waited for; matrix products, arithmetic and copies ran while one was open for 4% of the time, Pallas kernels for 0%

profile of v1, /device:TPU:0, one launch (start us, length us, event | category | flops | bytes accessed | tf_op | source)
XLA Modules:
  0.0 1484.0 jit_solution(11157764345537505490)
XLA Ops:
  7.2 5.2 stack.2
  12.4 11.7 all-to-all-start
  39.0 5.1 copy.79
  44.2 4.2 reshape.243
  49.5 75.7 %all-to-all-done = bf16[128,32,1024]{2,1,0:T(8,128)(2,1)} async-done(((bf16[128,32,1024]{2,1,0:T(8,128)(2,1)}), bf16[128,32,1024]{2,1,0:T(8,128)(2,1)}, u32[]{:S(2)}, u32[]{:S(2)}) %all-to-all-start) | async-done | bytes 8388640 | tf_op jit(solution)/shard_map/all_to_all | solution.py:65
  125.2 4.6 fusion.28
  147.3 190.5 %while.38 = (s32[]{:T(128)}, bf16[128,1024]{0,1:T(8,128)(2,1)}, bf16[16,128,1024]{1,2,0:T(8,128)(2,1)}, f32[4,2048,1]{1,0,2:T(4,128)S(1)}, f32[4,2048,1]{1,0,2:T...) while((s32[]{:T(128)}, bf16[128,1024]{0,1:T(8,128)(2,1)}, ...), condition=%wide.region_7.8_spmd.clone, body=%wide.region_2.7_spmd.clone.sunk | while | flops 551063552 | bytes 61154760 | solution.py:152
  150.6 13.7 collective-permute-start
  166.4 6.5 collective-permute-start
  175.0 16.2 %collective-permute-start = (bf16[128,1024]{0,1:T(8,128)(2,1)}, bf16[128,1024]{0,1:T(8,128)(2,1)S(1)}, u32[]{:S(2)}, u32[]{:S(2)}) collective-permute-start(bf16[128,1024]{0,1:T(8,128)(2,1)} %get-tuple-element.838), channel_id=1, source_target_pairs={{0,1},{1,2},{2,3},{3,4},{4,5},{5,6},{6,7},{7,8},{8,9},{9,10},{10,1... | collective-permute-start | bytes 786440 | tf_op jit(solution)/shard_map/while/body/eval_jaxpr/ppermute | solution.py:13
  193.3 6.5 collective-permute-start
  201.8 15.8 %collective-permute-start = (bf16[128,1024]{0,1:T(8,128)(2,1)}, bf16[128,1024]{0,1:T(8,128)(2,1)S(1)}, u32[]{:S(2)}, u32[]{:S(2)}) collective-permute-start(bf16[128,1024]{0,1:T(8,128)(2,1)} %get-tuple-element.838), channel_id=1, source_target_pairs={{0,1},{1,2},{2,3},{3,4},{4,5},{5,6},{6,7},{7,8},{8,9},{9,10},{10,1... | collective-permute-start | bytes 786440 | tf_op jit(solution)/shard_map/while/body/eval_jaxpr/ppermute | solution.py:13
  219.7 7.4 collective-permute-start
  229.2 17.1 %collective-permute-start = (bf16[128,1024]{0,1:T(8,128)(2,1)}, bf16[128,1024]{0,1:T(8,128)(2,1)S(1)}, u32[]{:S(2)}, u32[]{:S(2)}) collective-permute-start(bf16[128,1024]{0,1:T(8,128)(2,1)} %get-tuple-element.838), channel_id=1, source_target_pairs={{0,1},{1,2},{2,3},{3,4},{4,5},{5,6},{6,7},{7,8},{8,9},{9,10},{10,1... | collective-permute-start | bytes 786440 | tf_op jit(solution)/shard_map/while/body/eval_jaxpr/ppermute | solution.py:13
  248.3 7.4 collective-permute-start
  257.8 11.1 collective-permute-start
  271.0 7.4 collective-permute-start
  280.5 17.1 %collective-permute-start = (bf16[128,1024]{0,1:T(8,128)(2,1)}, bf16[128,1024]{0,1:T(8,128)(2,1)S(1)}, u32[]{:S(2)}, u32[]{:S(2)}) collective-permute-start(bf16[128,1024]{0,1:T(8,128)(2,1)} %get-tuple-element.838), channel_id=1, source_target_pairs={{0,1},{1,2},{2,3},{3,4},{4,5},{5,6},{6,7},{7,8},{8,9},{9,10},{10,1... | collective-permute-start | bytes 786440 | tf_op jit(solution)/shard_map/while/body/eval_jaxpr/ppermute | solution.py:13
  299.6 7.4 collective-permute-start
  309.1 17.0 %collective-permute-start = (bf16[128,1024]{0,1:T(8,128)(2,1)}, bf16[128,1024]{0,1:T(8,128)(2,1)S(1)}, u32[]{:S(2)}, u32[]{:S(2)}) collective-permute-start(bf16[128,1024]{0,1:T(8,128)(2,1)} %get-tuple-element.838), channel_id=1, source_target_pairs={{0,1},{1,2},{2,3},{3,4},{4,5},{5,6},{6,7},{7,8},{8,9},{9,10},{10,1... | collective-permute-start | bytes 786440 | tf_op jit(solution)/shard_map/while/body/eval_jaxpr/ppermute | solution.py:13
  328.2 7.4 collective-permute-start
  337.7 5.4 copy.77
  343.2 5.0 multiply_reduce_fusion
  350.4 436.3 %while.39 = (s32[]{:T(128)}, f32[128,1024]{0,1:T(8,128)}, f32[4,2048,128]{2,1,0:T(8,128)}, s32[]{:T(128)}, bf16[16,128,1024]{1,2,0:T(8,128)(2,1)}, /*index=5*/bf...) while((s32[]{:T(128)}, f32[128,1024]{0,1:T(8,128)}, ...), condition=%wide.region_12.13_spmd.clone, body=%wide.region_9.12_spmd.clone.sunk | while | flops 1351823360 | bytes 85468640 | solution.py:212
  351.3 11.4 conditional.7
  363.7 15.2 %collective-permute-start.1 = (bf16[128,1024]{0,1:T(8,128)(2,1)S(1)}, bf16[128,1024]{0,1:T(8,128)(2,1)}, u32[]{:S(2)}, u32[]{:S(2)}) collective-permute-start(bf16[128,1024]{0,1:T(8,128)(2,1)S(1)} %convert_element_type.130), channel_id=1, source_target_pairs={{0,1},{1,2},{2,3},{3,4},{4,5},{5,6},{6,7},{7,8},{8,9},{9,10},{10,1... | collective-permute-start | bytes 786440 | tf_op jit(solution)/shard_map/while/body/eval_jaxpr/ppermute | solution.py:19
  379.0 82.2 %collective-permute-done.1 = bf16[128,1024]{0,1:T(8,128)(2,1)} collective-permute-done((bf16[128,1024]{0,1:T(8,128)(2,1)S(1)}, bf16[128,1024]{0,1:T(8,128)(2,1)}, u32[]{:S(2)}, u32[]{:S(2)}) %collective-permute-start.1) | collective-permute-done | bytes 262176 | tf_op jit(solution)/shard_map/while/body/eval_jaxpr/ppermute | solution.py:19
  466.1 14.7 collective-permute-done.1
  485.6 14.7 collective-permute-done.1
  505.2 14.7 collective-permute-done.1
  524.8 16.2 %collective-permute-done.1 = bf16[128,1024]{0,1:T(8,128)(2,1)} collective-permute-done((bf16[128,1024]{0,1:T(8,128)(2,1)S(1)}, bf16[128,1024]{0,1:T(8,128)(2,1)}, u32[]{:S(2)}, u32[]{:S(2)}) %collective-permute-start.1) | collective-permute-done | bytes 262176 | tf_op jit(solution)/shard_map/while/body/eval_jaxpr/ppermute | solution.py:19
  545.9 17.3 %collective-permute-done.1 = bf16[128,1024]{0,1:T(8,128)(2,1)} collective-permute-done((bf16[128,1024]{0,1:T(8,128)(2,1)S(1)}, bf16[128,1024]{0,1:T(8,128)(2,1)}, u32[]{:S(2)}, u32[]{:S(2)}) %collective-permute-start.1) | collective-permute-done | bytes 262176 | tf_op jit(solution)/shard_map/while/body/eval_jaxpr/ppermute | solution.py:19
  568.1 17.3 %collective-permute-done.1 = bf16[128,1024]{0,1:T(8,128)(2,1)} collective-permute-done((bf16[128,1024]{0,1:T(8,128)(2,1)S(1)}, bf16[128,1024]{0,1:T(8,128)(2,1)}, u32[]{:S(2)}, u32[]{:S(2)}) %collective-permute-start.1) | collective-permute-done | bytes 262176 | tf_op jit(solution)/shard_map/while/body/eval_jaxpr/ppermute | solution.py:19
  590.2 17.3 %collective-permute-done.1 = bf16[128,1024]{0,1:T(8,128)(2,1)} collective-permute-done((bf16[128,1024]{0,1:T(8,128)(2,1)S(1)}, bf16[128,1024]{0,1:T(8,128)(2,1)}, u32[]{:S(2)}, u32[]{:S(2)}) %collective-permute-start.1) | collective-permute-done | bytes 262176 | tf_op jit(solution)/shard_map/while/body/eval_jaxpr/ppermute | solution.py:19
  612.4 17.3 %collective-permute-done.1 = bf16[128,1024]{0,1:T(8,128)(2,1)} collective-permute-done((bf16[128,1024]{0,1:T(8,128)(2,1)S(1)}, bf16[128,1024]{0,1:T(8,128)(2,1)}, u32[]{:S(2)}, u32[]{:S(2)}) %collective-permute-start.1) | collective-permute-done | bytes 262176 | tf_op jit(solution)/shard_map/while/body/eval_jaxpr/ppermute | solution.py:19
  634.6 17.3 %collective-permute-done.1 = bf16[128,1024]{0,1:T(8,128)(2,1)} collective-permute-done((bf16[128,1024]{0,1:T(8,128)(2,1)S(1)}, bf16[128,1024]{0,1:T(8,128)(2,1)}, u32[]{:S(2)}, u32[]{:S(2)}) %collective-permute-start.1) | collective-permute-done | bytes 262176 | tf_op jit(solution)/shard_map/while/body/eval_jaxpr/ppermute | solution.py:19
  656.8 17.3 %collective-permute-done.1 = bf16[128,1024]{0,1:T(8,128)(2,1)} collective-permute-done((bf16[128,1024]{0,1:T(8,128)(2,1)S(1)}, bf16[128,1024]{0,1:T(8,128)(2,1)}, u32[]{:S(2)}, u32[]{:S(2)}) %collective-permute-start.1) | collective-permute-done | bytes 262176 | tf_op jit(solution)/shard_map/while/body/eval_jaxpr/ppermute | solution.py:19
  678.9 17.3 %collective-permute-done.1 = bf16[128,1024]{0,1:T(8,128)(2,1)} collective-permute-done((bf16[128,1024]{0,1:T(8,128)(2,1)S(1)}, bf16[128,1024]{0,1:T(8,128)(2,1)}, u32[]{:S(2)}, u32[]{:S(2)}) %collective-permute-start.1) | collective-permute-done | bytes 262176 | tf_op jit(solution)/shard_map/while/body/eval_jaxpr/ppermute | solution.py:19
  701.1 17.3 %collective-permute-done.1 = bf16[128,1024]{0,1:T(8,128)(2,1)} collective-permute-done((bf16[128,1024]{0,1:T(8,128)(2,1)S(1)}, bf16[128,1024]{0,1:T(8,128)(2,1)}, u32[]{:S(2)}, u32[]{:S(2)}) %collective-permute-start.1) | collective-permute-done | bytes 262176 | tf_op jit(solution)/shard_map/while/body/eval_jaxpr/ppermute | solution.py:19
  723.3 17.3 %collective-permute-done.1 = bf16[128,1024]{0,1:T(8,128)(2,1)} collective-permute-done((bf16[128,1024]{0,1:T(8,128)(2,1)S(1)}, bf16[128,1024]{0,1:T(8,128)(2,1)}, u32[]{:S(2)}, u32[]{:S(2)}) %collective-permute-start.1) | collective-permute-done | bytes 262176 | tf_op jit(solution)/shard_map/while/body/eval_jaxpr/ppermute | solution.py:19
  745.4 17.3 %collective-permute-done.1 = bf16[128,1024]{0,1:T(8,128)(2,1)} collective-permute-done((bf16[128,1024]{0,1:T(8,128)(2,1)S(1)}, bf16[128,1024]{0,1:T(8,128)(2,1)}, u32[]{:S(2)}, u32[]{:S(2)}) %collective-permute-start.1) | collective-permute-done | bytes 262176 | tf_op jit(solution)/shard_map/while/body/eval_jaxpr/ppermute | solution.py:19
  767.6 17.3 %collective-permute-done.1 = bf16[128,1024]{0,1:T(8,128)(2,1)} collective-permute-done((bf16[128,1024]{0,1:T(8,128)(2,1)S(1)}, bf16[128,1024]{0,1:T(8,128)(2,1)}, u32[]{:S(2)}, u32[]{:S(2)}) %collective-permute-start.1) | collective-permute-done | bytes 262176 | tf_op jit(solution)/shard_map/while/body/eval_jaxpr/ppermute | solution.py:19
  790.2 8.1 convolution_bitcast_fusion
  798.2 17.4 %copy.98 = f32[4096,1024]{1,0:T(8,128)} copy(f32[4096,1024]{0,1:T(8,128)} %convolution_bitcast_fusion) | data formatting | bytes 33554432
  821.7 4.2 broadcast_in_dim_reshape.3
  831.2 4.2 convert_element_type.98
  835.3 7.3 fusion.22
  842.6 634.6 %reduce-scatter.4.cloned.1.call-done = f32[32,1024]{1,0:T(8,128)} async-done(((f32[4096,1024]{1,0:T(8,128)}), f32[32,1024]{1,0:T(8,128)}) %reduce-scatter.4.cloned.1.call-update) | async-done | bytes 131088
  (290 shorter events, 170.0 us)
Async XLA Ops:
  7.2 118.0 %copy-start = (bf16[1,128,4096]{2,1,0:T(8,128)(2,1)S(1)}, bf16[1,128,4096]{2,1,0:T(8,128)(2,1)}, u32[]{:S(2)}) copy-start(bf16[1,128,4096]{2,1,0:T(8,128)(2,1)} %param.12) | copy-start | bytes 3145732
  12.4 112.8 %all-to-all-start = ((bf16[128,32,1024]{2,1,0:T(8,128)(2,1)}), bf16[128,32,1024]{2,1,0:T(8,128)(2,1)}, u32[]{:S(2)}, u32[]{:S(2)}) async-start(bf16[128,32,1024]{2,1,0:T(8,128)(2,1)} %stack.2), calls=%async_computation | async-start | bytes 16777216 | tf_op jit(solution)/shard_map/all_to_all | solution.py:65
  24.1 1453.0 %reduce-scatter.4.cloned.1.call-start = ((), (), s32[]{:S(2)}) async-start(), calls=%async_computation.2 | async-start | bytes 16908288
  48.7 84.0 %copy-start.10 = (f32[128,64]{1,0:T(8,128)}, f32[128,64]{1,0:T(8,128)S(1)}, u32[]{:S(2)}) copy-start(f32[128,64]{1,0:T(8,128)S(1)} %get-tuple-element.695) | copy-start | bytes 98308
  48.7 84.0 %copy-start.11 = (f32[128,64]{1,0:T(8,128)}, f32[128,64]{1,0:T(8,128)S(1)}, u32[]{:S(2)}) copy-start(f32[128,64]{1,0:T(8,128)S(1)} %get-tuple-element.696) | copy-start | bytes 98308
  129.8 0.8 copy-start.7
  138.2 2.9 copy-start.8
  144.3 0.9 copy-start.9
  145.3 2.0 copy-start.6
  147.3 2.6 collective-permute-start
  150.6 15.1 %collective-permute-start = (bf16[128,1024]{0,1:T(8,128)(2,1)}, bf16[128,1024]{0,1:T(8,128)(2,1)S(1)}, u32[]{:S(2)}, u32[]{:S(2)}) collective-permute-start(bf16[128,1024]{0,1:T(8,128)(2,1)} %get-tuple-element.838), channel_id=1, source_target_pairs={{0,1},{1,2},{2,3},{3,4},{4,5},{5,6},{6,7},{7,8},{8,9},{9,10},{10,1... | collective-permute-start | bytes 786440 | tf_op jit(solution)/shard_map/while/body/eval_jaxpr/ppermute | solution.py:13
  166.4 7.9 collective-permute-start
  175.0 17.5 %collective-permute-start = (bf16[128,1024]{0,1:T(8,128)(2,1)}, bf16[128,1024]{0,1:T(8,128)(2,1)S(1)}, u32[]{:S(2)}, u32[]{:S(2)}) collective-permute-start(bf16[128,1024]{0,1:T(8,128)(2,1)} %get-tuple-element.838), channel_id=1, source_target_pairs={{0,1},{1,2},{2,3},{3,4},{4,5},{5,6},{6,7},{7,8},{8,9},{9,10},{10,1... | collective-permute-start | bytes 786440 | tf_op jit(solution)/shard_map/while/body/eval_jaxpr/ppermute | solution.py:13
  193.3 7.9 collective-permute-start
  201.8 17.2 %collective-permute-start = (bf16[128,1024]{0,1:T(8,128)(2,1)}, bf16[128,1024]{0,1:T(8,128)(2,1)S(1)}, u32[]{:S(2)}, u32[]{:S(2)}) collective-permute-start(bf16[128,1024]{0,1:T(8,128)(2,1)} %get-tuple-element.838), channel_id=1, source_target_pairs={{0,1},{1,2},{2,3},{3,4},{4,5},{5,6},{6,7},{7,8},{8,9},{9,10},{10,1... | collective-permute-start | bytes 786440 | tf_op jit(solution)/shard_map/while/body/eval_jaxpr/ppermute | solution.py:13
  219.7 8.8 collective-permute-start
  229.2 18.4 %collective-permute-start = (bf16[128,1024]{0,1:T(8,128)(2,1)}, bf16[128,1024]{0,1:T(8,128)(2,1)S(1)}, u32[]{:S(2)}, u32[]{:S(2)}) collective-permute-start(bf16[128,1024]{0,1:T(8,128)(2,1)} %get-tuple-element.838), channel_id=1, source_target_pairs={{0,1},{1,2},{2,3},{3,4},{4,5},{5,6},{6,7},{7,8},{8,9},{9,10},{10,1... | collective-permute-start | bytes 786440 | tf_op jit(solution)/shard_map/while/body/eval_jaxpr/ppermute | solution.py:13
  248.3 8.8 collective-permute-start
  257.8 12.5 collective-permute-start
  271.0 8.8 collective-permute-start
  280.5 18.4 %collective-permute-start = (bf16[128,1024]{0,1:T(8,128)(2,1)}, bf16[128,1024]{0,1:T(8,128)(2,1)S(1)}, u32[]{:S(2)}, u32[]{:S(2)}) collective-permute-start(bf16[128,1024]{0,1:T(8,128)(2,1)} %get-tuple-element.838), channel_id=1, source_target_pairs={{0,1},{1,2},{2,3},{3,4},{4,5},{5,6},{6,7},{7,8},{8,9},{9,10},{10,1... | collective-permute-start | bytes 786440 | tf_op jit(solution)/shard_map/while/body/eval_jaxpr/ppermute | solution.py:13
  299.6 8.8 collective-permute-start
  309.1 18.4 %collective-permute-start = (bf16[128,1024]{0,1:T(8,128)(2,1)}, bf16[128,1024]{0,1:T(8,128)(2,1)S(1)}, u32[]{:S(2)}, u32[]{:S(2)}) collective-permute-start(bf16[128,1024]{0,1:T(8,128)(2,1)} %get-tuple-element.838), channel_id=1, source_target_pairs={{0,1},{1,2},{2,3},{3,4},{4,5},{5,6},{6,7},{7,8},{8,9},{9,10},{10,1... | collective-permute-start | bytes 786440 | tf_op jit(solution)/shard_map/while/body/eval_jaxpr/ppermute | solution.py:13
  328.2 8.8 collective-permute-start
  351.3 2.8 copy-start.1
  355.6 3.0 copy-start.4
  360.7 1.9 copy-start.5
  363.7 97.5 %collective-permute-start.1 = (bf16[128,1024]{0,1:T(8,128)(2,1)S(1)}, bf16[128,1024]{0,1:T(8,128)(2,1)}, u32[]{:S(2)}, u32[]{:S(2)}) collective-permute-start(bf16[128,1024]{0,1:T(8,128)(2,1)S(1)} %convert_element_type.130), channel_id=1, source_target_pairs={{0,1},{1,2},{2,3},{3,4},{4,5},{5,6},{6,7},{7,8},{8,9},{9,10},{10,1... | collective-permute-start | bytes 786440 | tf_op jit(solution)/shard_map/while/body/eval_jaxpr/ppermute | solution.py:19
  466.0 14.8 collective-permute-start.1
  485.6 14.8 collective-permute-start.1
  505.1 14.8 collective-permute-start.1
  524.7 16.3 %collective-permute-start.1 = (bf16[128,1024]{0,1:T(8,128)(2,1)S(1)}, bf16[128,1024]{0,1:T(8,128)(2,1)}, u32[]{:S(2)}, u32[]{:S(2)}) collective-permute-start(bf16[128,1024]{0,1:T(8,128)(2,1)S(1)} %convert_element_type.130), channel_id=1, source_target_pairs={{0,1},{1,2},{2,3},{3,4},{4,5},{5,6},{6,7},{7,8},{8,9},{9,10},{10,1... | collective-permute-start | bytes 786440 | tf_op jit(solution)/shard_map/while/body/eval_jaxpr/ppermute | solution.py:19
  545.8 17.4 %collective-permute-start.1 = (bf16[128,1024]{0,1:T(8,128)(2,1)S(1)}, bf16[128,1024]{0,1:T(8,128)(2,1)}, u32[]{:S(2)}, u32[]{:S(2)}) collective-permute-start(bf16[128,1024]{0,1:T(8,128)(2,1)S(1)} %convert_element_type.130), channel_id=1, source_target_pairs={{0,1},{1,2},{2,3},{3,4},{4,5},{5,6},{6,7},{7,8},{8,9},{9,10},{10,1... | collective-permute-start | bytes 786440 | tf_op jit(solution)/shard_map/while/body/eval_jaxpr/ppermute | solution.py:19
  568.0 17.4 %collective-permute-start.1 = (bf16[128,1024]{0,1:T(8,128)(2,1)S(1)}, bf16[128,1024]{0,1:T(8,128)(2,1)}, u32[]{:S(2)}, u32[]{:S(2)}) collective-permute-start(bf16[128,1024]{0,1:T(8,128)(2,1)S(1)} %convert_element_type.130), channel_id=1, source_target_pairs={{0,1},{1,2},{2,3},{3,4},{4,5},{5,6},{6,7},{7,8},{8,9},{9,10},{10,1... | collective-permute-start | bytes 786440 | tf_op jit(solution)/shard_map/while/body/eval_jaxpr/ppermute | solution.py:19
  590.2 17.4 %collective-permute-start.1 = (bf16[128,1024]{0,1:T(8,128)(2,1)S(1)}, bf16[128,1024]{0,1:T(8,128)(2,1)}, u32[]{:S(2)}, u32[]{:S(2)}) collective-permute-start(bf16[128,1024]{0,1:T(8,128)(2,1)S(1)} %convert_element_type.130), channel_id=1, source_target_pairs={{0,1},{1,2},{2,3},{3,4},{4,5},{5,6},{6,7},{7,8},{8,9},{9,10},{10,1... | collective-permute-start | bytes 786440 | tf_op jit(solution)/shard_map/while/body/eval_jaxpr/ppermute | solution.py:19
  612.3 17.4 %collective-permute-start.1 = (bf16[128,1024]{0,1:T(8,128)(2,1)S(1)}, bf16[128,1024]{0,1:T(8,128)(2,1)}, u32[]{:S(2)}, u32[]{:S(2)}) collective-permute-start(bf16[128,1024]{0,1:T(8,128)(2,1)S(1)} %convert_element_type.130), channel_id=1, source_target_pairs={{0,1},{1,2},{2,3},{3,4},{4,5},{5,6},{6,7},{7,8},{8,9},{9,10},{10,1... | collective-permute-start | bytes 786440 | tf_op jit(solution)/shard_map/while/body/eval_jaxpr/ppermute | solution.py:19
  634.5 17.4 %collective-permute-start.1 = (bf16[128,1024]{0,1:T(8,128)(2,1)S(1)}, bf16[128,1024]{0,1:T(8,128)(2,1)}, u32[]{:S(2)}, u32[]{:S(2)}) collective-permute-start(bf16[128,1024]{0,1:T(8,128)(2,1)S(1)} %convert_element_type.130), channel_id=1, source_target_pairs={{0,1},{1,2},{2,3},{3,4},{4,5},{5,6},{6,7},{7,8},{8,9},{9,10},{10,1... | collective-permute-start | bytes 786440 | tf_op jit(solution)/shard_map/while/body/eval_jaxpr/ppermute | solution.py:19
  656.7 17.4 %collective-permute-start.1 = (bf16[128,1024]{0,1:T(8,128)(2,1)S(1)}, bf16[128,1024]{0,1:T(8,128)(2,1)}, u32[]{:S(2)}, u32[]{:S(2)}) collective-permute-start(bf16[128,1024]{0,1:T(8,128)(2,1)S(1)} %convert_element_type.130), channel_id=1, source_target_pairs={{0,1},{1,2},{2,3},{3,4},{4,5},{5,6},{6,7},{7,8},{8,9},{9,10},{10,1... | collective-permute-start | bytes 786440 | tf_op jit(solution)/shard_map/while/body/eval_jaxpr/ppermute | solution.py:19
  678.8 17.4 %collective-permute-start.1 = (bf16[128,1024]{0,1:T(8,128)(2,1)S(1)}, bf16[128,1024]{0,1:T(8,128)(2,1)}, u32[]{:S(2)}, u32[]{:S(2)}) collective-permute-start(bf16[128,1024]{0,1:T(8,128)(2,1)S(1)} %convert_element_type.130), channel_id=1, source_target_pairs={{0,1},{1,2},{2,3},{3,4},{4,5},{5,6},{6,7},{7,8},{8,9},{9,10},{10,1... | collective-permute-start | bytes 786440 | tf_op jit(solution)/shard_map/while/body/eval_jaxpr/ppermute | solution.py:19
  701.0 17.4 %collective-permute-start.1 = (bf16[128,1024]{0,1:T(8,128)(2,1)S(1)}, bf16[128,1024]{0,1:T(8,128)(2,1)}, u32[]{:S(2)}, u32[]{:S(2)}) collective-permute-start(bf16[128,1024]{0,1:T(8,128)(2,1)S(1)} %convert_element_type.130), channel_id=1, source_target_pairs={{0,1},{1,2},{2,3},{3,4},{4,5},{5,6},{6,7},{7,8},{8,9},{9,10},{10,1... | collective-permute-start | bytes 786440 | tf_op jit(solution)/shard_map/while/body/eval_jaxpr/ppermute | solution.py:19
  723.2 17.4 %collective-permute-start.1 = (bf16[128,1024]{0,1:T(8,128)(2,1)S(1)}, bf16[128,1024]{0,1:T(8,128)(2,1)}, u32[]{:S(2)}, u32[]{:S(2)}) collective-permute-start(bf16[128,1024]{0,1:T(8,128)(2,1)S(1)} %convert_element_type.130), channel_id=1, source_target_pairs={{0,1},{1,2},{2,3},{3,4},{4,5},{5,6},{6,7},{7,8},{8,9},{9,10},{10,1... | collective-permute-start | bytes 786440 | tf_op jit(solution)/shard_map/while/body/eval_jaxpr/ppermute | solution.py:19
  745.4 17.4 %collective-permute-start.1 = (bf16[128,1024]{0,1:T(8,128)(2,1)S(1)}, bf16[128,1024]{0,1:T(8,128)(2,1)}, u32[]{:S(2)}, u32[]{:S(2)}) collective-permute-start(bf16[128,1024]{0,1:T(8,128)(2,1)S(1)} %convert_element_type.130), channel_id=1, source_target_pairs={{0,1},{1,2},{2,3},{3,4},{4,5},{5,6},{6,7},{7,8},{8,9},{9,10},{10,1... | collective-permute-start | bytes 786440 | tf_op jit(solution)/shard_map/while/body/eval_jaxpr/ppermute | solution.py:19
  767.5 17.4 %collective-permute-start.1 = (bf16[128,1024]{0,1:T(8,128)(2,1)S(1)}, bf16[128,1024]{0,1:T(8,128)(2,1)}, u32[]{:S(2)}, u32[]{:S(2)}) collective-permute-start(bf16[128,1024]{0,1:T(8,128)(2,1)S(1)} %convert_element_type.130), channel_id=1, source_target_pairs={{0,1},{1,2},{2,3},{3,4},{4,5},{5,6},{6,7},{7,8},{8,9},{9,10},{10,1... | collective-permute-start | bytes 786440 | tf_op jit(solution)/shard_map/while/body/eval_jaxpr/ppermute | solution.py:19
Sparse Core Ops, SparseCore 0:
  815.8 661.2 reduce-scatter.3
